TPU v7x, 256 devices: a whole 4x4x8 slice. The times are simulated.
256 devices in a mesh: ctx: 64 (over z, y, core), tsp: 4 (over x).
Axes of the slice: x: 4, y: 4, z: 8, core: 2. Of those that a mesh axis runs over, the one named last changes fastest.
Arguments:
- queries: bfloat16 [32768, 5120], P(('ctx', 'tsp')), may hold values from -6 to 6
- keys: bfloat16 [32768, 5120], P(('ctx', 'tsp')), may hold values from -6 to 6
- values: bfloat16 [32768, 5120], P(('ctx', 'tsp')), may hold values from -6 to 6
- cotangent: bfloat16 [32768, 5120], P(('ctx', 'tsp')), may hold values from -6 to 6
- content_bias: float32 [40, 128], P('tsp'), may hold values from -5 to 5
- memory_lengths: int32 [64], P('ctx'), may hold values from 0 to 1536, as said below
- segment_ends: int32 [64], P('ctx'), may hold values from 1 to 512, as said below
Outputs:
- attended: bfloat16 [32768, 5120], P(('ctx', 'tsp'))
- grad_queries: bfloat16 [32768, 5120], P(('ctx', 'tsp'))
- grad_keys: bfloat16 [32768, 5120], P(('ctx', 'tsp'))
- grad_values: bfloat16 [32768, 5120], P(('ctx', 'tsp'))
- grad_bias: float32 [40, 128], P('tsp')
Inputs may be any that keep to these rules, and one draw needn't show every extreme that they name: memory_lengths[0] is 0 and the last shard's value is 1536. `segment_ends`: a value of 512 means that the shard's first document runs to its end; shard 1 has the value 1 and the last shard the value 512.
All inputs are finite; a program needn't handle non-finite values.
Results may differ from a plain program's by a relative error of at most 0.012.
The roundings to bfloat16 on the way count: a program that leaves them out, or rounds other values in their place, can miss the bound.
Values may be sent and summed in bfloat16 or wider, within the bound.
A program may use at most 128 MiB of HBM per device.

v0:
```python
import math
import jax
import jax.numpy as jnp
from jax import lax
from jax.sharding import PartitionSpec as P

MEM = 1536


def passed_along(value, axis, steps):
    count = lax.axis_size(axis)
    initial, last = (max(0, -steps), min(count, count - steps))
    return lax.ppermute(value, axis, [(source, source + steps) for source in range(initial, last)])


def column_block(matrix, first_col, count):
    return lax.dynamic_slice_in_dim(matrix, first_col, count, 1)


def merge_heads(piece_stack):
    head_total, tok_rows, head_size = piece_stack.shape
    return jnp.transpose(piece_stack, (1, 0, 2)).reshape(tok_rows, head_total * head_size)


def shards(queries, keys, values, cotangent, content_bias, memory_lengths, segment_ends):
    q_heads, k_heads, v_heads, g_heads = (
        lax.all_to_all(queries, "tsp", split_axis=1, concat_axis=0, tiled=True),
        lax.all_to_all(keys, "tsp", split_axis=1, concat_axis=0, tiled=True),
        lax.all_to_all(values, "tsp", split_axis=1, concat_axis=0, tiled=True),
        lax.all_to_all(cotangent, "tsp", split_axis=1, concat_axis=0, tiled=True),
    )
    tok_rows = q_heads.shape[0]
    local_heads = content_bias.shape[0]
    head_size = content_bias.shape[1]
    shard_count = (MEM + tok_rows - 1) // tok_rows
    stacked = jnp.stack([k_heads, v_heads])
    blocks = []
    current = stacked
    for stride in range(shard_count):
        current = passed_along(current, "ctx", 1)
        blocks = [current] + blocks
    window = jnp.concatenate(blocks, axis=1)
    position = lax.axis_index("ctx")
    usable = jnp.minimum(memory_lengths[0], position * tok_rows)
    boundary = segment_ends[0]
    span_rows = MEM + tok_rows
    row_index = lax.broadcasted_iota(jnp.int32, (tok_rows, span_rows), 0)
    col_index = lax.broadcasted_iota(jnp.int32, (tok_rows, span_rows), 1)
    offset = col_index - MEM
    memory_ok = (col_index < MEM) & (col_index >= MEM - usable) & (row_index < boundary)
    local_ok = (
        (col_index >= MEM) & (offset <= row_index) & ((row_index < boundary) == (offset < boundary))
    )
    allowed = memory_ok | local_ok
    scaling = 1.0 / math.sqrt(head_size)
    contract_cols = (((1,), (1,)), ((), ()))
    contract_rows = (((0,), (0,)), ((), ()))

    def one_head(head_index):
        first_col = head_index * head_size
        query_rows = column_block(q_heads, first_col, head_size)
        head_bias = lax.dynamic_slice_in_dim(content_bias, head_index, 1, 0)
        shifted = (query_rows.astype(jnp.float32) + head_bias).astype(jnp.bfloat16)
        key_rows = jnp.concatenate(
            [
                column_block(window[0], first_col, head_size),
                column_block(k_heads, first_col, head_size),
            ],
            axis=0,
        )
        value_rows = jnp.concatenate(
            [
                column_block(window[1], first_col, head_size),
                column_block(v_heads, first_col, head_size),
            ],
            axis=0,
        )
        grad_rows = column_block(g_heads, first_col, head_size)
        scores = (
            lax.dot_general(shifted, key_rows, contract_cols, preferred_element_type=jnp.float32)
            * scaling
        )
        scores = jnp.where(allowed, scores, -jnp.inf)
        row_peak = jnp.max(scores, axis=1, keepdims=True)
        weights = jnp.exp(scores - row_peak)
        probs_full = weights / jnp.sum(weights, axis=1, keepdims=True)
        probs_half = probs_full.astype(jnp.bfloat16)
        attended = jnp.dot(probs_half, value_rows, preferred_element_type=jnp.float32).astype(
            jnp.bfloat16
        )
        grad_probs = lax.dot_general(
            grad_rows, value_rows, contract_cols, preferred_element_type=jnp.float32
        )
        centre = jnp.sum(probs_full * grad_probs, axis=1, keepdims=True)
        grad_scores = (probs_full * (grad_probs - centre) * scaling).astype(jnp.bfloat16)
        grad_query = jnp.dot(grad_scores, key_rows, preferred_element_type=jnp.float32)
        grad_key = lax.dot_general(
            grad_scores[:, MEM:], shifted, contract_rows, preferred_element_type=jnp.float32
        ).astype(jnp.bfloat16)
        grad_value = lax.dot_general(
            probs_half[:, MEM:], grad_rows, contract_rows, preferred_element_type=jnp.float32
        ).astype(jnp.bfloat16)
        return (
            attended,
            grad_query.astype(jnp.bfloat16),
            grad_key,
            grad_value,
            jnp.sum(grad_query, axis=0),
        )

    results = lax.map(one_head, jnp.arange(local_heads, dtype=jnp.int32))
    attended = merge_heads(results[0])
    grad_queries = merge_heads(results[1])
    grad_keys = merge_heads(results[2])
    grad_values = merge_heads(results[3])
    grad_bias = lax.psum(results[4], "ctx")
    outputs = (
        lax.all_to_all(attended, "tsp", split_axis=0, concat_axis=1, tiled=True),
        lax.all_to_all(grad_queries, "tsp", split_axis=0, concat_axis=1, tiled=True),
        lax.all_to_all(grad_keys, "tsp", split_axis=0, concat_axis=1, tiled=True),
        lax.all_to_all(grad_values, "tsp", split_axis=0, concat_axis=1, tiled=True),
    )
    return (outputs[0], outputs[1], outputs[2], outputs[3], grad_bias)


def solution(mesh):
    return jax.shard_map(
        shards,
        mesh=mesh,
        in_specs=(
            P(("ctx", "tsp"), None),
            P(("ctx", "tsp"), None),
            P(("ctx", "tsp"), None),
            P(("ctx", "tsp"), None),
            P("tsp", None),
            P("ctx"),
            P("ctx"),
        ),
        out_specs=(
            P(("ctx", "tsp"), None),
            P(("ctx", "tsp"), None),
            P(("ctx", "tsp"), None),
            P(("ctx", "tsp"), None),
            P("tsp", None),
        ),
        check_vma=False,
    )
```

profile of v0, /device:TPU:1, one launch (start us, length us, event | category | flops | bytes accessed | tf_op | source)
XLA Modules:
  0.0 595.5 jit_solution(16991121875115040467)
XLA Ops:
  0.6 2.6 copy.66
  3.2 4.8 all-to-all-start.1
  8.1 15.4 %all-to-all-done.1 = bf16[128,4,1280]{2,0,1:T(8,128)(2,1)} async-done(((bf16[128,4,1280]{2,0,1:T(8,128)(2,1)}), bf16[128,4,1280]{2,0,1:T(8,128)(2,1)}, u32[]{:S(2)}, u32[]{:S(2)}) %all-to-all-start.1) | async-done | bytes 1310752 | tf_op jit(solution)/shard_map/all_to_all | solution.py:28
  23.5 17.3 %all_to_all.152 = bf16[128,4,1280]{2,0,1:T(8,128)(2,1)} all-to-all(bf16[128,4,1280]{2,0,1:T(8,128)(2,1)S(1)} %bitcast.107), channel_id=1, replica_groups=mesh['ctx'=64,'tsp'=4] {'tsp'}, dimensions={1} | all-to-all | bytes 2621440 | tf_op jit(solution)/shard_map/all_to_all | solution.py:29
  42.8 10.0 %collective-permute-start = (bf16[2,512,1280]{2,1,0:T(8,128)(2,1)S(1)}, bf16[2,512,1280]{2,1,0:T(8,128)(2,1)S(1)}, u32[]{:S(2)}, u32[]{:S(2)}) collective-permute-start(bf16[2,512,1280]{2,1,0:T(8,128)(2,1)S(1)} %pad_maximum_fusion.7), channel_id=1, source_target_pairs={{0,4},{4,8},{8,12},{12,16},{16,20},{20,24},{24,28},{28,32},{32,36}... | collective-permute-start | bytes 7864328 | tf_op jit(solution)/shard_map/ppermute | solution.py:13
  52.9 28.6 %collective-permute-done = bf16[2,512,1280]{2,1,0:T(8,128)(2,1)S(1)} collective-permute-done((bf16[2,512,1280]{2,1,0:T(8,128)(2,1)S(1)}, bf16[2,512,1280]{2,1,0:T(8,128)(2,1)S(1)}, u32[]{:S(2)}, u32[]{:S(2)}) %collective-permute-start) | collective-permute-done | bytes 2621472 | tf_op jit(solution)/shard_map/ppermute | solution.py:13
  81.4 4.4 collective-permute-start.1
  85.8 28.6 %collective-permute-done.1 = bf16[2,512,1280]{2,1,0:T(8,128)(2,1)} collective-permute-done((bf16[2,512,1280]{2,1,0:T(8,128)(2,1)S(1)}, bf16[2,512,1280]{2,1,0:T(8,128)(2,1)}, u32[]{:S(2)}, u32[]{:S(2)}) %collective-permute-start.1) | collective-permute-done | bytes 2621472 | tf_op jit(solution)/shard_map/ppermute | solution.py:13
  114.4 4.5 collective-permute-start.2
  120.1 4.3 all-to-all-start
  128.3 14.5 %all-to-all-done = bf16[128,4,1280]{2,0,1:T(8,128)(2,1)} async-done(((bf16[128,4,1280]{2,0,1:T(8,128)(2,1)}), bf16[128,4,1280]{2,0,1:T(8,128)(2,1)}, u32[]{:S(2)}, u32[]{:S(2)}) %all-to-all-start) | async-done | bytes 1310752 | tf_op jit(solution)/shard_map/all_to_all | solution.py:27
  142.8 4.3 all-to-all-start.3
  147.8 6.2 %pad_maximum_fusion.6 = bf16[2,1536,1280]{2,1,0:T(8,128)(2,1)} fusion(bf16[2,512,1280]{2,1,0:T(8,128)(2,1)S(1)} %collective-permute-done, bf16[2,512,1280]{2,1,0:T(8,128)(2,1)} %collective-permute-done.1, bf16[2,512,1280]{2,1,0:T(8,128)(2,1)} %collective-permute-done.2), kind=kLoop, calls=%fused_computation.45 | loop fusion | flops 23592960 | bytes 15728640 | tf_op jit(solution)/shard_map/concatenate | solution.py:42
  154.0 10.8 %all-to-all-done.3 = bf16[128,4,1280]{2,0,1:T(8,128)(2,1)} async-done(((bf16[128,4,1280]{2,0,1:T(8,128)(2,1)}), bf16[128,4,1280]{2,0,1:T(8,128)(2,1)}, u32[]{:S(2)}, u32[]{:S(2)}) %all-to-all-start.3) | async-done | bytes 1310752 | tf_op jit(solution)/shard_map/all_to_all | solution.py:30
  164.8 226.8 %while.19 = (s32[]{:T(128)}, bf16[10,512,128]{2,1,0:T(8,128)(2,1)}, bf16[10,512,128]{2,1,0:T(8,128)(2,1)}, bf16[10,512,128]{2,1,0:T(8,128)(2,1)}, bf16[10,512,12...) while((s32[]{:T(128)}, bf16[10,512,128]{2,1,0:T(8,128)(2,1)}, ...), condition=%wide.region_5.6_spmd.clone, body=%wide.region_0.5_spmd.clone.sunk | while | flops 1235941760 | bytes 64526704 | solution.py:111
  166.0 3.6 fusion.51
  173.3 2.9 fusion.53
  188.7 3.6 fusion.51
  196.0 2.9 fusion.53
  211.4 3.6 fusion.51
  218.6 2.9 fusion.53
  234.0 3.6 fusion.51
  241.3 2.9 fusion.53
  256.7 3.6 fusion.51
  264.0 2.9 fusion.53
  279.4 3.6 fusion.51
  286.6 2.9 fusion.53
  302.0 3.6 fusion.51
  309.3 2.9 fusion.53
  324.7 3.6 fusion.51
  332.0 2.9 fusion.53
  347.4 3.6 fusion.51
  354.7 2.9 fusion.53
  370.1 3.6 fusion.51
  377.4 2.9 fusion.53
  394.7 3.5 all-to-all-start.4
  401.1 2.6 copy.47
  403.7 11.3 %all-to-all-done.4 = bf16[4,128,1280]{1,2,0:T(8,128)(2,1)S(1)} async-done(((bf16[4,128,1280]{1,2,0:T(8,128)(2,1)}), bf16[4,128,1280]{1,2,0:T(8,128)(2,1)S(1)}, u32[]{:S(2)}, u32[]{:S(2)}) %all-to-all-start.4) | async-done | bytes 1310752 | tf_op jit(solution)/shard_map/all_to_all | solution.py:118
  414.9 3.5 all-to-all-start.5
  420.9 3.6 all_to_all.136
  424.5 2.5 copy.49
  427.0 7.2 %all-to-all-done.5 = bf16[4,128,1280]{1,2,0:T(8,128)(2,1)S(1)} async-done(((bf16[4,128,1280]{1,2,0:T(8,128)(2,1)}), bf16[4,128,1280]{1,2,0:T(8,128)(2,1)S(1)}, u32[]{:S(2)}, u32[]{:S(2)}) %all-to-all-start.5) | async-done | bytes 1310752 | tf_op jit(solution)/shard_map/all_to_all | solution.py:119
  434.2 4.5 all-to-all-start.6
  441.2 3.6 all_to_all.140
  444.7 2.5 copy.51
  447.3 5.9 all-to-all-done.6
  453.2 4.3 all-to-all-start.7
  457.5 130.3 %psum.7 = f32[10,128]{1,0:T(8,128)} all-reduce(f32[10,128]{1,0:T(8,128)S(1)} %get-tuple-element.85), channel_id=1, replica_groups=mesh['ctx'=64,'tsp'=4] {'ctx'}, use_global_device_ids=true, to_apply=%region_6.7 | all-reduce | flops 1280 | bytes 10240 | tf_op jit(solution)/shard_map/psum | solution.py:116
  (181 shorter events, 160.9 us)
Async XLA Ops:
  0.6 7.4 %copy-start.1 = (bf16[128,5120]{1,0:T(8,128)(2,1)S(1)}, bf16[128,5120]{1,0:T(8,128)(2,1)}, u32[]{:S(2)}) copy-start(bf16[128,5120]{1,0:T(8,128)(2,1)} %param.11) | copy-start | bytes 3932164
  3.2 20.3 %all-to-all-start.1 = ((bf16[128,4,1280]{2,0,1:T(8,128)(2,1)}), bf16[128,4,1280]{2,0,1:T(8,128)(2,1)}, u32[]{:S(2)}, u32[]{:S(2)}) async-start(bf16[128,4,1280]{2,0,1:T(8,128)(2,1)} %bitcast.80), calls=%async_computation.1 | async-start | bytes 2621440 | tf_op jit(solution)/shard_map/all_to_all | solution.py:28
  40.8 78.1 %copy-start.2 = (bf16[128,5120]{1,0:T(8,128)(2,1)S(1)}, bf16[128,5120]{1,0:T(8,128)(2,1)}, u32[]{:S(2)}) copy-start(bf16[128,5120]{1,0:T(8,128)(2,1)} %param.9) | copy-start | bytes 3932164
  42.8 38.6 %collective-permute-start = (bf16[2,512,1280]{2,1,0:T(8,128)(2,1)S(1)}, bf16[2,512,1280]{2,1,0:T(8,128)(2,1)S(1)}, u32[]{:S(2)}, u32[]{:S(2)}) collective-permute-start(bf16[2,512,1280]{2,1,0:T(8,128)(2,1)S(1)} %pad_maximum_fusion.7), channel_id=1, source_target_pairs={{0,4},{4,8},{8,12},{12,16},{16,20},{20,24},{24,28},{28,32},{32,36}... | collective-permute-start | bytes 7864328 | tf_op jit(solution)/shard_map/ppermute | solution.py:13
  81.4 33.0 %collective-permute-start.1 = (bf16[2,512,1280]{2,1,0:T(8,128)(2,1)S(1)}, bf16[2,512,1280]{2,1,0:T(8,128)(2,1)}, u32[]{:S(2)}, u32[]{:S(2)}) collective-permute-start(bf16[2,512,1280]{2,1,0:T(8,128)(2,1)S(1)} %collective-permute-done), channel_id=1, source_target_pairs={{0,4},{4,8},{8,12},{12,16},{16,20},{20,24},{24,28},{28,32},{32,36}... | collective-permute-start | bytes 7864328 | tf_op jit(solution)/shard_map/ppermute | solution.py:13
  114.4 33.4 %collective-permute-start.2 = (bf16[2,512,1280]{2,1,0:T(8,128)(2,1)}, bf16[2,512,1280]{2,1,0:T(8,128)(2,1)}, u32[]{:S(2)}, u32[]{:S(2)}) collective-permute-start(bf16[2,512,1280]{2,1,0:T(8,128)(2,1)} %collective-permute-done.1), channel_id=1, source_target_pairs={{0,4},{4,8},{8,12},{12,16},{16,20},{20,24},{24,28},{28,32},{32,36}... | collective-permute-start | bytes 7864328 | tf_op jit(solution)/shard_map/ppermute | solution.py:13
  120.1 22.7 %all-to-all-start = ((bf16[128,4,1280]{2,0,1:T(8,128)(2,1)}), bf16[128,4,1280]{2,0,1:T(8,128)(2,1)}, u32[]{:S(2)}, u32[]{:S(2)}) async-start(bf16[128,4,1280]{2,0,1:T(8,128)(2,1)} %bitcast.81), calls=%async_computation | async-start | bytes 2621440 | tf_op jit(solution)/shard_map/all_to_all | solution.py:27
  142.8 22.0 %all-to-all-start.3 = ((bf16[128,4,1280]{2,0,1:T(8,128)(2,1)}), bf16[128,4,1280]{2,0,1:T(8,128)(2,1)}, u32[]{:S(2)}, u32[]{:S(2)}) async-start(bf16[128,4,1280]{2,0,1:T(8,128)(2,1)} %bitcast.78), calls=%async_computation.3 | async-start | bytes 2621440 | tf_op jit(solution)/shard_map/all_to_all | solution.py:30
  180.6 1.5 copy-start
  203.2 1.4 copy-start
  225.9 1.4 copy-start
  248.5 1.4 copy-start
  271.2 1.4 copy-start
  293.9 1.4 copy-start
  316.5 1.4 copy-start
  339.2 1.5 copy-start
  361.9 1.5 copy-start
  384.6 1.5 copy-start
  394.7 20.2 %all-to-all-start.4 = ((bf16[4,128,1280]{1,2,0:T(8,128)(2,1)}), bf16[4,128,1280]{1,2,0:T(8,128)(2,1)S(1)}, u32[]{:S(2)}, u32[]{:S(2)}) async-start(bf16[4,128,1280]{1,2,0:T(8,128)(2,1)} %copy.45), calls=%async_computation.4 | async-start | bytes 2621440 | tf_op jit(solution)/shard_map/all_to_all | solution.py:118
  414.9 19.3 %all-to-all-start.5 = ((bf16[4,128,1280]{1,2,0:T(8,128)(2,1)}), bf16[4,128,1280]{1,2,0:T(8,128)(2,1)S(1)}, u32[]{:S(2)}, u32[]{:S(2)}) async-start(bf16[4,128,1280]{1,2,0:T(8,128)(2,1)} %copy.47), calls=%async_computation.5 | async-start | bytes 2621440 | tf_op jit(solution)/shard_map/all_to_all | solution.py:119
  434.2 18.9 %all-to-all-start.6 = ((bf16[4,128,1280]{1,2,0:T(8,128)(2,1)}), bf16[4,128,1280]{1,2,0:T(8,128)(2,1)}, u32[]{:S(2)}, u32[]{:S(2)}) async-start(bf16[4,128,1280]{1,2,0:T(8,128)(2,1)} %copy.49), calls=%async_computation.6 | async-start | bytes 2621440 | tf_op jit(solution)/shard_map/all_to_all | solution.py:120
  453.2 139.9 %all-to-all-start.7 = ((bf16[4,128,1280]{1,2,0:T(8,128)(2,1)}), bf16[4,128,1280]{1,2,0:T(8,128)(2,1)}, u32[]{:S(2)}, u32[]{:S(2)}) async-start(bf16[4,128,1280]{1,2,0:T(8,128)(2,1)} %copy.51), calls=%async_computation.7 | async-start | bytes 2621440 | tf_op jit(solution)/shard_map/all_to_all | solution.py:121
where the time goes:
time: 598 us; the launch traced here: 595 us
  blocking collectives  148 us (25%)
  waiting for transfers between devices  123 us (21%)
  matrix products  118 us (20%)
  local copies, waits for them, and re-layouts  99.6 us (17%)
  starting transfers between devices  48.2 us (8%)
  other arithmetic  31.5 us (5%)
  loops' own time  25.9 us (4%)
    psum x1, blocking collectives, shards(): grad_bias = lax.psum(results[4], 'ctx')  130 us
    ppermute x3, waiting for transfers between devices, passed_along(): lax.ppermute(value, axis, [(source, source + steps) for source in range(i...  57.9 us
    slice x10, local copies, waits for them, and re-layouts, one_head(): window[1]  36 us
    dot_general x10, matrix products, one_head(): lax.dot_general(shifted, key_rows, contract_cols, preferred_element_type=...  29.1 us
    another operation x1, loops' own time, shards(): results = lax.map(one_head, jnp.arange(local_heads, dtype=jnp.int32))  25.9 us
    dot_general x10, matrix products, one_head(): lax.dot_general(grad_scores[:, MEM:], shifted, contract_rows, preferred_e...  20.8 us
    dot_general x10, matrix products, one_head(): lax.dot_general(grad_rows, value_rows, contract_cols, preferred_element_t...  20.7 us
    dot_general x10, matrix products, one_head(): lax.dot_general(probs_half[:, MEM:], grad_rows, contract_rows, preferred_...  19.1 us
  transfers between devices with their start and end apart: 10, of which 9 were waited for; matrix products, arithmetic and copies ran while one was open for 5% of the time, Pallas kernels for 0%

commit v1 on v0

--- a/solution.py
+++ b/solution.py
@@ -113,7 +113,7 @@
     grad_queries = merge_heads(results[1])
     grad_keys = merge_heads(results[2])
     grad_values = merge_heads(results[3])
-    grad_bias = lax.psum(results[4], "ctx")
+    grad_bias = jnp.sum(lax.all_gather(results[4], "ctx"), axis=0)
     outputs = (
         lax.all_to_all(attended, "tsp", split_axis=0, concat_axis=1, tiled=True),
         lax.all_to_all(grad_queries, "tsp", split_axis=0, concat_axis=1, tiled=True),

time: 598 us -> 526 us (0.88)
  blocking collectives: 148 us -> 74.2 us
    psum x1 -> x0, blocking collectives: 130 us -> none  [shards(): grad_bias = lax.psum(results[4], 'ctx')]
    all_gather x0 -> x1, blocking collectives: none -> 56.9 us  [shards(): grad_bias = jnp.sum(lax.all_gather(results[4], 'ctx'), axis=0)]
  transfers between devices with their start and end apart: 10 -> 10, of which waited for: 9 -> 9; matrix products, arithmetic and copies ran while one was open for 5% -> 6% of each run, Pallas kernels for 0% -> 0%
where the time goes in v1:
time: 526 us; the launch traced here: 523 us
  waiting for transfers between devices  123 us (23%)
  matrix products  118 us (22%)
  local copies, waits for them, and re-layouts  99.6 us (19%)
  blocking collectives  74.2 us (14%)
  starting transfers between devices  48.2 us (9%)
  other arithmetic  32.2 us (6%)
  loops' own time  25.9 us (5%)
    ppermute x3, waiting for transfers between devices, passed_along(): lax.ppermute(value, axis, [(source, source + steps) for source in range(i...  57.9 us
    all_gather x1, blocking collectives, shards(): grad_bias = jnp.sum(lax.all_gather(results[4], 'ctx'), axis=0)  56.9 us
    slice x10, local copies, waits for them, and re-layouts, one_head(): window[1]  36 us
    dot_general x10, matrix products, one_head(): lax.dot_general(shifted, key_rows, contract_cols, preferred_element_type=...  29.1 us
    another operation x1, loops' own time, shards(): results = lax.map(one_head, jnp.arange(local_heads, dtype=jnp.int32))  25.9 us
    dot_general x10, matrix products, one_head(): lax.dot_general(grad_scores[:, MEM:], shifted, contract_rows, preferred_e...  20.8 us
    dot_general x10, matrix products, one_head(): lax.dot_general(grad_rows, value_rows, contract_cols, preferred_element_t...  20.8 us
    dot_general x10, matrix products, one_head(): lax.dot_general(probs_half[:, MEM:], grad_rows, contract_rows, preferred_...  19.1 us
  transfers between devices with their start and end apart: 10, of which 9 were waited for; matrix products, arithmetic and copies ran while one was open for 6% of the time, Pallas kernels for 0%

profile of v1, /device:TPU:1, one launch (start us, length us, event | category | flops | bytes accessed | tf_op | source)
XLA Modules:
  0.0 522.8 jit_solution(8765145533249923163)
XLA Ops:
  0.6 2.6 copy.66
  3.2 4.8 all-to-all-start.1
  8.1 15.4 %all-to-all-done.1 = bf16[128,4,1280]{2,0,1:T(8,128)(2,1)} async-done(((bf16[128,4,1280]{2,0,1:T(8,128)(2,1)}), bf16[128,4,1280]{2,0,1:T(8,128)(2,1)}, u32[]{:S(2)}, u32[]{:S(2)}) %all-to-all-start.1) | async-done | bytes 1310752 | tf_op jit(solution)/shard_map/all_to_all | solution.py:28
  23.5 17.3 %all_to_all.152 = bf16[128,4,1280]{2,0,1:T(8,128)(2,1)} all-to-all(bf16[128,4,1280]{2,0,1:T(8,128)(2,1)S(1)} %bitcast.108), channel_id=1, replica_groups=mesh['ctx'=64,'tsp'=4] {'tsp'}, dimensions={1} | all-to-all | bytes 2621440 | tf_op jit(solution)/shard_map/all_to_all | solution.py:29
  42.8 10.0 %collective-permute-start = (bf16[2,512,1280]{2,1,0:T(8,128)(2,1)S(1)}, bf16[2,512,1280]{2,1,0:T(8,128)(2,1)S(1)}, u32[]{:S(2)}, u32[]{:S(2)}) collective-permute-start(bf16[2,512,1280]{2,1,0:T(8,128)(2,1)S(1)} %pad_maximum_fusion.7), channel_id=1, source_target_pairs={{0,4},{4,8},{8,12},{12,16},{16,20},{20,24},{24,28},{28,32},{32,36}... | collective-permute-start | bytes 7864328 | tf_op jit(solution)/shard_map/ppermute | solution.py:13
  52.9 28.6 %collective-permute-done = bf16[2,512,1280]{2,1,0:T(8,128)(2,1)S(1)} collective-permute-done((bf16[2,512,1280]{2,1,0:T(8,128)(2,1)S(1)}, bf16[2,512,1280]{2,1,0:T(8,128)(2,1)S(1)}, u32[]{:S(2)}, u32[]{:S(2)}) %collective-permute-start) | collective-permute-done | bytes 2621472 | tf_op jit(solution)/shard_map/ppermute | solution.py:13
  81.4 4.4 collective-permute-start.1
  85.8 28.6 %collective-permute-done.1 = bf16[2,512,1280]{2,1,0:T(8,128)(2,1)} collective-permute-done((bf16[2,512,1280]{2,1,0:T(8,128)(2,1)S(1)}, bf16[2,512,1280]{2,1,0:T(8,128)(2,1)}, u32[]{:S(2)}, u32[]{:S(2)}) %collective-permute-start.1) | collective-permute-done | bytes 2621472 | tf_op jit(solution)/shard_map/ppermute | solution.py:13
  114.4 4.5 collective-permute-start.2
  120.1 4.3 all-to-all-start
  128.3 14.5 %all-to-all-done = bf16[128,4,1280]{2,0,1:T(8,128)(2,1)} async-done(((bf16[128,4,1280]{2,0,1:T(8,128)(2,1)}), bf16[128,4,1280]{2,0,1:T(8,128)(2,1)}, u32[]{:S(2)}, u32[]{:S(2)}) %all-to-all-start) | async-done | bytes 1310752 | tf_op jit(solution)/shard_map/all_to_all | solution.py:27
  142.8 4.3 all-to-all-start.3
  147.8 6.2 %pad_maximum_fusion.6 = bf16[2,1536,1280]{2,1,0:T(8,128)(2,1)} fusion(bf16[2,512,1280]{2,1,0:T(8,128)(2,1)S(1)} %collective-permute-done, bf16[2,512,1280]{2,1,0:T(8,128)(2,1)} %collective-permute-done.1, bf16[2,512,1280]{2,1,0:T(8,128)(2,1)} %collective-permute-done.2), kind=kLoop, calls=%fused_computation.45 | loop fusion | flops 23592960 | bytes 15728640 | tf_op jit(solution)/shard_map/concatenate | solution.py:42
  154.0 10.8 %all-to-all-done.3 = bf16[128,4,1280]{2,0,1:T(8,128)(2,1)} async-done(((bf16[128,4,1280]{2,0,1:T(8,128)(2,1)}), bf16[128,4,1280]{2,0,1:T(8,128)(2,1)}, u32[]{:S(2)}, u32[]{:S(2)}) %all-to-all-start.3) | async-done | bytes 1310752 | tf_op jit(solution)/shard_map/all_to_all | solution.py:30
  164.8 226.9 %while.19 = (s32[]{:T(128)}, bf16[10,512,128]{2,1,0:T(8,128)(2,1)}, bf16[10,512,128]{2,1,0:T(8,128)(2,1)}, bf16[10,512,128]{2,1,0:T(8,128)(2,1)}, bf16[10,512,12...) while((s32[]{:T(128)}, bf16[10,512,128]{2,1,0:T(8,128)(2,1)}, ...), condition=%wide.region_5.6_spmd.clone, body=%wide.region_0.5_spmd.clone.sunk | while | flops 1235941760 | bytes 64526704 | solution.py:111
  166.0 3.6 fusion.51
  173.3 2.9 fusion.53
  188.7 3.6 fusion.51
  196.0 2.9 fusion.53
  211.4 3.6 fusion.51
  218.7 2.9 fusion.53
  234.1 3.6 fusion.51
  241.3 2.9 fusion.53
  256.8 3.6 fusion.51
  264.0 2.9 fusion.53
  279.4 3.6 fusion.51
  286.7 2.9 fusion.53
  302.1 3.6 fusion.51
  309.4 2.9 fusion.53
  324.8 3.6 fusion.51
  332.1 2.9 fusion.53
  347.5 3.6 fusion.51
  354.8 2.9 fusion.53
  370.2 3.6 fusion.51
  377.5 2.9 fusion.53
  394.8 3.5 all-to-all-start.4
  401.2 2.6 copy.47
  403.8 11.3 %all-to-all-done.4 = bf16[4,128,1280]{1,2,0:T(8,128)(2,1)S(1)} async-done(((bf16[4,128,1280]{1,2,0:T(8,128)(2,1)}), bf16[4,128,1280]{1,2,0:T(8,128)(2,1)S(1)}, u32[]{:S(2)}, u32[]{:S(2)}) %all-to-all-start.4) | async-done | bytes 1310752 | tf_op jit(solution)/shard_map/all_to_all | solution.py:118
  415.0 3.5 all-to-all-start.5
  421.0 3.6 all_to_all.136
  424.6 2.5 copy.49
  427.1 7.2 %all-to-all-done.5 = bf16[4,128,1280]{1,2,0:T(8,128)(2,1)S(1)} async-done(((bf16[4,128,1280]{1,2,0:T(8,128)(2,1)}), bf16[4,128,1280]{1,2,0:T(8,128)(2,1)S(1)}, u32[]{:S(2)}, u32[]{:S(2)}) %all-to-all-start.5) | async-done | bytes 1310752 | tf_op jit(solution)/shard_map/all_to_all | solution.py:119
  434.3 4.5 all-to-all-start.6
  441.2 3.6 all_to_all.140
  444.8 2.5 copy.51
  447.3 5.9 %all-to-all-done.6 = bf16[4,128,1280]{1,2,0:T(8,128)(2,1)} async-done(((bf16[4,128,1280]{1,2,0:T(8,128)(2,1)}), bf16[4,128,1280]{1,2,0:T(8,128)(2,1)}, u32[]{:S(2)}, u32[]{:S(2)}) %all-to-all-start.6) | async-done | bytes 1310752 | tf_op jit(solution)/shard_map/all_to_all | solution.py:120
  453.2 4.3 all-to-all-start.7
  457.5 56.9 %all-gather.1 = f32[64,10,128]{2,1,0:T(8,128)S(1)} all-gather(f32[1,10,128]{2,1,0:T(8,128)S(1)} %bitcast.118), channel_id=2, replica_groups=mesh['ctx'=64,'tsp'=4] {'ctx'}, dimensions={0}, use_global_device_ids=true | all-gather | bytes 332800 | tf_op jit(solution)/shard_map/all_gather | solution.py:116
  (182 shorter events, 161.7 us)
Async XLA Ops:
  0.6 7.4 %copy-start.1 = (bf16[128,5120]{1,0:T(8,128)(2,1)S(1)}, bf16[128,5120]{1,0:T(8,128)(2,1)}, u32[]{:S(2)}) copy-start(bf16[128,5120]{1,0:T(8,128)(2,1)} %param.11) | copy-start | bytes 3932164
  3.2 20.3 %all-to-all-start.1 = ((bf16[128,4,1280]{2,0,1:T(8,128)(2,1)}), bf16[128,4,1280]{2,0,1:T(8,128)(2,1)}, u32[]{:S(2)}, u32[]{:S(2)}) async-start(bf16[128,4,1280]{2,0,1:T(8,128)(2,1)} %bitcast.81), calls=%async_computation.1 | async-start | bytes 2621440 | tf_op jit(solution)/shard_map/all_to_all | solution.py:28
  40.8 78.1 %copy-start.2 = (bf16[128,5120]{1,0:T(8,128)(2,1)S(1)}, bf16[128,5120]{1,0:T(8,128)(2,1)}, u32[]{:S(2)}) copy-start(bf16[128,5120]{1,0:T(8,128)(2,1)} %param.9) | copy-start | bytes 3932164
  42.8 38.6 %collective-permute-start = (bf16[2,512,1280]{2,1,0:T(8,128)(2,1)S(1)}, bf16[2,512,1280]{2,1,0:T(8,128)(2,1)S(1)}, u32[]{:S(2)}, u32[]{:S(2)}) collective-permute-start(bf16[2,512,1280]{2,1,0:T(8,128)(2,1)S(1)} %pad_maximum_fusion.7), channel_id=1, source_target_pairs={{0,4},{4,8},{8,12},{12,16},{16,20},{20,24},{24,28},{28,32},{32,36}... | collective-permute-start | bytes 7864328 | tf_op jit(solution)/shard_map/ppermute | solution.py:13
  81.4 33.0 %collective-permute-start.1 = (bf16[2,512,1280]{2,1,0:T(8,128)(2,1)S(1)}, bf16[2,512,1280]{2,1,0:T(8,128)(2,1)}, u32[]{:S(2)}, u32[]{:S(2)}) collective-permute-start(bf16[2,512,1280]{2,1,0:T(8,128)(2,1)S(1)} %collective-permute-done), channel_id=1, source_target_pairs={{0,4},{4,8},{8,12},{12,16},{16,20},{20,24},{24,28},{28,32},{32,36}... | collective-permute-start | bytes 7864328 | tf_op jit(solution)/shard_map/ppermute | solution.py:13
  114.4 33.4 %collective-permute-start.2 = (bf16[2,512,1280]{2,1,0:T(8,128)(2,1)}, bf16[2,512,1280]{2,1,0:T(8,128)(2,1)}, u32[]{:S(2)}, u32[]{:S(2)}) collective-permute-start(bf16[2,512,1280]{2,1,0:T(8,128)(2,1)} %collective-permute-done.1), channel_id=1, source_target_pairs={{0,4},{4,8},{8,12},{12,16},{16,20},{20,24},{24,28},{28,32},{32,36}... | collective-permute-start | bytes 7864328 | tf_op jit(solution)/shard_map/ppermute | solution.py:13
  120.1 22.7 %all-to-all-start = ((bf16[128,4,1280]{2,0,1:T(8,128)(2,1)}), bf16[128,4,1280]{2,0,1:T(8,128)(2,1)}, u32[]{:S(2)}, u32[]{:S(2)}) async-start(bf16[128,4,1280]{2,0,1:T(8,128)(2,1)} %bitcast.82), calls=%async_computation | async-start | bytes 2621440 | tf_op jit(solution)/shard_map/all_to_all | solution.py:27
  142.8 22.0 %all-to-all-start.3 = ((bf16[128,4,1280]{2,0,1:T(8,128)(2,1)}), bf16[128,4,1280]{2,0,1:T(8,128)(2,1)}, u32[]{:S(2)}, u32[]{:S(2)}) async-start(bf16[128,4,1280]{2,0,1:T(8,128)(2,1)} %bitcast.79), calls=%async_computation.3 | async-start | bytes 2621440 | tf_op jit(solution)/shard_map/all_to_all | solution.py:30
  180.5 1.5 copy-start
  203.2 1.4 copy-start
  225.9 1.4 copy-start
  248.6 1.4 copy-start
  271.3 1.4 copy-start
  293.9 1.4 copy-start
  316.6 1.4 copy-start
  339.3 1.5 copy-start
  362.0 1.5 copy-start
  384.7 1.5 copy-start
  394.8 20.2 %all-to-all-start.4 = ((bf16[4,128,1280]{1,2,0:T(8,128)(2,1)}), bf16[4,128,1280]{1,2,0:T(8,128)(2,1)S(1)}, u32[]{:S(2)}, u32[]{:S(2)}) async-start(bf16[4,128,1280]{1,2,0:T(8,128)(2,1)} %copy.45), calls=%async_computation.4 | async-start | bytes 2621440 | tf_op jit(solution)/shard_map/all_to_all | solution.py:118
  415.0 19.3 %all-to-all-start.5 = ((bf16[4,128,1280]{1,2,0:T(8,128)(2,1)}), bf16[4,128,1280]{1,2,0:T(8,128)(2,1)S(1)}, u32[]{:S(2)}, u32[]{:S(2)}) async-start(bf16[4,128,1280]{1,2,0:T(8,128)(2,1)} %copy.47), calls=%async_computation.5 | async-start | bytes 2621440 | tf_op jit(solution)/shard_map/all_to_all | solution.py:119
  434.3 18.9 %all-to-all-start.6 = ((bf16[4,128,1280]{1,2,0:T(8,128)(2,1)}), bf16[4,128,1280]{1,2,0:T(8,128)(2,1)}, u32[]{:S(2)}, u32[]{:S(2)}) async-start(bf16[4,128,1280]{1,2,0:T(8,128)(2,1)} %copy.49), calls=%async_computation.6 | async-start | bytes 2621440 | tf_op jit(solution)/shard_map/all_to_all | solution.py:120
  453.2 67.2 %all-to-all-start.7 = ((bf16[4,128,1280]{1,2,0:T(8,128)(2,1)}), bf16[4,128,1280]{1,2,0:T(8,128)(2,1)}, u32[]{:S(2)}, u32[]{:S(2)}) async-start(bf16[4,128,1280]{1,2,0:T(8,128)(2,1)} %copy.51), calls=%async_computation.7 | async-start | bytes 2621440 | tf_op jit(solution)/shard_map/all_to_all | solution.py:121
